TPU v7x, 256 devices: a whole 4x4x8 slice. The times are simulated.
256 devices in a mesh: ex: 8 (over z_lo, core), ey: 32 (over z_hi, x, y).
Axes of the slice: x: 4, y: 4, z: 8 (z_hi: 2, z_lo: 4; z = z_hi * 4 + z_lo), core: 2. Of those that a mesh axis runs over, the one named last changes fastest.
Arguments:
- tokens: bfloat16 [256, 256, 1024], P(('ex', 'ey')), may hold values from -16 to 16
- slot_param: bfloat16 [1024, 64], replicated, may hold values from -0.75 to 0.75
- weight_in: bfloat16 [64, 1024, 4096], P('ey', None, 'ex'), may hold values from -0.1875 to 0.1875
- weight_out: bfloat16 [64, 4096, 1024], P('ey', 'ex'), may hold values from -0.09375 to 0.09375
- grad_out: bfloat16 [256, 256, 1024], P(('ex', 'ey')), may hold values from -6 to 6
Outputs:
- grad_tokens: bfloat16 [256, 256, 1024], P(('ex', 'ey'))
- grad_param: float32 [1024, 64], replicated
- grad_win: bfloat16 [64, 1024, 4096], P('ey', None, 'ex')
- grad_wout: bfloat16 [64, 4096, 1024], P('ey', 'ex')
All inputs are finite; a program needn't handle non-finite values.
Results may differ from a plain program's by a relative error of at most 0.017.
Values may be sent and summed in bfloat16 or wider, within the bound.
A program may use at most 64 MiB of HBM per device.

v0:
```python
import jax
import jax.numpy as jnp
from jax import lax
from jax.sharding import Mesh
from jax.sharding import PartitionSpec as P

EX = ("ex_0", "ex_1")
EX_EY = ("ex_0", "ex_1", "ey")


def sum_in_order(tiles, axes, sequence):
    inside = tiles.shape[1:]
    tiles = tiles.reshape(*(lax.axis_size(a) for a in axes), *inside)
    tiles = jnp.moveaxis(tiles, sequence, range(len(axes))).reshape(-1, *inside)
    for k in sequence:
        tiles = lax.psum_scatter(tiles, axes[k], scatter_dimension=0, tiled=True)
    return tiles[0]


def in_blocks(array, dim, length):
    before, after = (array.shape[:dim], array.shape[dim + 1 :])
    return jnp.moveaxis(array.reshape(*before, length, -1, *after), dim, 0)


def summed_rows(array, axes, sequence, dim):
    length = lax.axis_size(axes)
    return sum_in_order(in_blocks(array, dim, length), axes, sequence)


def gelu_parts(pre):
    cdf = 0.5 * (1.0 + lax.erf(pre * 0.7071067811865476))
    slope = cdf + pre * jnp.exp(-0.5 * pre * pre) * 0.3989422804014327
    return (pre * cdf, slope)


def softmax_along(values, axis):
    top = jnp.max(values, axis=axis, keepdims=True)
    expo = jnp.exp(values - top)
    return expo / jnp.sum(expo, axis=axis, keepdims=True)


def route_in(stacked):
    moved = lax.all_to_all(stacked, "ey", split_axis=2, concat_axis=0, tiled=True)
    return lax.all_gather(moved, EX, axis=0, tiled=True)


def route_out(term_fn, total_rows):
    summed = summed_rows(
        term_fn(jnp.int32(0), total_rows // lax.axis_size(EX) * lax.axis_size(EX)).astype(
            jnp.bfloat16
        ),
        EX,
        (1, 0),
        0,
    ).astype(jnp.float32)
    return lax.all_to_all(
        summed.astype(jnp.bfloat16), "ey", split_axis=0, concat_axis=2, tiled=True
    )


def per_device(tokens, slot_param, weight_in, weight_out, grad_out):
    logits = jnp.einsum("ipd,ds->ips", tokens, slot_param, preferred_element_type=jnp.float32)
    dispatch = softmax_along(logits, 1)
    combine = softmax_along(logits, 2)
    dispatch_b = dispatch.astype(jnp.bfloat16)
    combine_b = combine.astype(jnp.bfloat16)
    slot_in = jnp.einsum(
        "ips,ipd->isd", dispatch_b, tokens, preferred_element_type=jnp.float32
    ).astype(jnp.bfloat16)
    slot_cot = jnp.einsum(
        "ips,ipd->isd", combine_b, grad_out, preferred_element_type=jnp.float32
    ).astype(jnp.bfloat16)
    arrived = route_in(jnp.stack((slot_in, slot_cot), axis=1))
    total_rows = arrived.shape[0]
    slot_x = arrived[:, 0]
    slot_g = arrived[:, 1]
    pre = jnp.einsum("red,edf->ref", slot_x, weight_in, preferred_element_type=jnp.float32)
    value, slope = gelu_parts(pre)
    hidden = value.astype(jnp.bfloat16)
    back = jnp.einsum("red,efd->ref", slot_g, weight_out, preferred_element_type=jnp.float32)
    dpre = (back * slope).astype(jnp.bfloat16)

    def paired_term(start, count):
        return jnp.concatenate(
            (
                jnp.einsum("ref,efd->red", hidden, weight_out, preferred_element_type=jnp.float32)[
                    :, None
                ],
                jnp.einsum("ref,edf->red", dpre, weight_in, preferred_element_type=jnp.float32)[
                    :, None
                ],
            ),
            axis=1,
        )

    paired = route_out(paired_term, total_rows)
    slot_out = paired[:, 0]
    grad_slot = paired[:, 1]
    grad_win = jnp.einsum("red,ref->edf", slot_x, dpre, preferred_element_type=jnp.float32).astype(
        jnp.bfloat16
    )
    grad_wout = jnp.einsum(
        "ref,red->efd", hidden, slot_g, preferred_element_type=jnp.float32
    ).astype(jnp.bfloat16)
    d_combine = jnp.einsum("ipd,isd->ips", grad_out, slot_out, preferred_element_type=jnp.float32)
    d_dispatch = jnp.einsum("ipd,isd->ips", tokens, grad_slot, preferred_element_type=jnp.float32)
    d_logits = dispatch * (d_dispatch - jnp.sum(dispatch * d_dispatch, axis=1, keepdims=True))
    d_logits = d_logits + combine * (
        d_combine - jnp.sum(combine * d_combine, axis=2, keepdims=True)
    )
    logit_grad = d_logits.astype(jnp.bfloat16)
    grad_tokens = jnp.einsum(
        "ips,isd->ipd", dispatch_b, grad_slot, preferred_element_type=jnp.float32
    )
    grad_tokens = grad_tokens + jnp.einsum(
        "ips,ds->ipd", logit_grad, slot_param, preferred_element_type=jnp.float32
    )
    local_param = jnp.einsum("ipd,ips->ds", tokens, logit_grad, preferred_element_type=jnp.float32)
    grad_param = lax.psum(local_param, EX_EY)
    return (grad_tokens.astype(jnp.bfloat16), grad_param, grad_win, grad_wout)


def solution(mesh):
    split = Mesh(mesh.devices.reshape(4, 2, mesh.shape["ey"]), ("ex_0", "ex_1", "ey"))
    return jax.shard_map(
        per_device,
        mesh=split,
        in_specs=(
            P(EX_EY, None, None),
            P(),
            P("ey", None, EX),
            P("ey", EX, None),
            P(EX_EY, None, None),
        ),
        out_specs=(P(EX_EY, None, None), P(), P("ey", None, EX), P("ey", EX, None)),
        check_vma=False,
    )
```

profile of v0, /device:TPU:2, one launch (start us, length us, event | category | flops | bytes accessed | tf_op | source)
XLA Modules:
  0.0 418.5 jit_solution(196067309297569867)
XLA Ops:
  7.2 1.6 fusion.34
  8.8 0.2 fusion.23
  9.0 1.3 fusion.4
  10.3 1.2 fusion.5
  11.6 0.3 copy.31
  11.9 25.9 %all_to_all.36 = bf16[1,2,64,1024]{3,1,0,2:T(2,128)(2,1)S(1)} all-to-all(bf16[1,2,64,1024]{3,1,0,2:T(2,128)(2,1)S(1)} %copy.31), channel_id=1, replica_groups=mesh['ex_0'=4,'ex_1'=2,'ey'=32] {'ey'}, dimensions={2} | all-to-all | bytes 524288 | tf_op jit(solution)/shard_map/all_to_all | solution.py:43
  37.8 0.8 copy.59
  38.6 0.0 reduce-scatter.3.cloned.1.call-start
  38.7 36.5 %all-gather.3.cloned.1.call-done = bf16[256,1,2,2,1024]{4,0,3,2,1:T(8,128)(2,1)} async-done(((bf16[32,1,2,2,1024]{4,0,3,2,1:T(8,128)(2,1)}), bf16[256,1,2,2,1024]{4,0,3,2,1:T(8,128)(2,1)}) %all-gather.3.cloned.1.call-update) | async-done | bytes 2097168 | tf_op jit(solution)/shard_map/all_gather | solution.py:44
  75.2 2.8 convolution_bitcast_fusion.1
  78.0 1.0 fusion.2
  79.0 0.7 convolution_convert_fusion.3
  79.7 1.0 copy-done.1
  80.7 0.7 convolution_convert_fusion.2
  81.5 0.2 pad_maximum_fusion
  81.7 1.5 copy.41
  83.3 14.7 %reduce-scatter.3.cloned.1.call-done = bf16[4,32,2,2,1024]{4,1,3,2,0:T(8,128)(2,1)} async-done(((bf16[8,32,2,2,1024]{4,1,3,2,0:T(8,128)(2,1)}), bf16[4,32,2,2,1024]{4,1,3,2,0:T(8,128)(2,1)}) %reduce-scatter.3.cloned.1.call-update) | async-done | bytes 1048592 | tf_op jit(solution)/shard_map/reduce_scatter | solution.py:16
  97.9 36.4 %reduce-scatter.5.cloned.1.call-done = bf16[1,32,2,2,1024]{4,1,3,2,0:T(8,128)(2,1)} async-done(((bf16[4,32,2,2,1024]{4,1,3,2,0:T(8,128)(2,1)}), bf16[1,32,2,2,1024]{4,1,3,2,0:T(8,128)(2,1)}) %reduce-scatter.5.cloned.1.call-update) | async-done | bytes 262160 | tf_op jit(solution)/shard_map/reduce_scatter | solution.py:16
  134.4 1.9 copy.35
  136.3 10.2 %all-to-all-start.1 = ((bf16[32,2,2,1024]{3,2,1,0:T(2,128)(2,1)}), bf16[32,2,2,1024]{3,2,1,0:T(2,128)(2,1)S(1)}, u32[]{:S(2)}, u32[]{:S(2)}) async-start(bf16[32,2,2,1024]{3,2,1,0:T(2,128)(2,1)} %copy.35), calls=%async_computation.3 | async-start | bytes 524288 | tf_op jit(solution)/shard_map/all_to_all | solution.py:56
  146.6 3.6 convolution_convert_fusion.1
  150.1 2.1 convolution_convert_fusion
  152.2 6.0 %all-to-all-done.1 = bf16[32,2,2,1024]{3,2,1,0:T(2,128)(2,1)S(1)} async-done(((bf16[32,2,2,1024]{3,2,1,0:T(2,128)(2,1)}), bf16[32,2,2,1024]{3,2,1,0:T(2,128)(2,1)S(1)}, u32[]{:S(2)}, u32[]{:S(2)}) %all-to-all-start.1) | async-done | bytes 262176 | tf_op jit(solution)/shard_map/all_to_all | solution.py:56
  158.3 0.2 copy.36
  158.5 0.4 fusion.35
  158.9 1.4 convolution_bitcast_fusion.3
  160.2 1.4 fusion.20
  161.6 0.4 multiply_reduce_fusion.1
  162.0 1.0 convolution_bitcast_fusion.2
  163.0 2.4 fusion.3
  165.4 244.9 %all-reduce.2.cloned.1.call-done = f32[1024,64]{0,1:T(8,128)} async-done(((f32[1024,64]{0,1:T(8,128)}), f32[1024,64]{0,1:T(8,128)}) %all-reduce.2.cloned.1.call-update) | async-done | bytes 262160 | tf_op jit(solution)/shard_map/psum | solution.py:119
  410.3 1.7 copy.61
  (21 shorter events, 0.3 us)
Async XLA Ops:
  7.2 70.8 %copy-start = (bf16[2,512,1024]{2,1,0:T(8,128)(2,1)S(1)}, bf16[2,512,1024]{2,1,0:T(8,128)(2,1)}, u32[]{:S(2)}) copy-start(bf16[2,512,1024]{2,1,0:T(8,128)(2,1)} %param.8) | copy-start | bytes 6291460
  7.2 68.0 %all-gather.3.cloned.1.call-start = ((), (), s32[]{:S(2)}) async-start(), calls=%async_computation.7 | async-start | bytes 2359296 | tf_op jit(solution)/shard_map/all_gather | solution.py:44
  38.6 59.3 %reduce-scatter.3.cloned.1.call-start = ((), (), s32[]{:S(2)}) async-start(), calls=%async_computation.4 | async-start | bytes 3145728 | tf_op jit(solution)/shard_map/reduce_scatter | solution.py:16
  75.2 2.8 copy-start.3
  79.0 2.5 copy-start.5
  79.0 1.8 copy-start.1
  83.2 51.2 %reduce-scatter.5.cloned.1.call-start = ((), (), s32[]{:S(2)}) async-start(), calls=%async_computation.5 | async-start | bytes 1310720 | tf_op jit(solution)/shard_map/reduce_scatter | solution.py:16
  136.3 21.9 %all-to-all-start.1 = ((bf16[32,2,2,1024]{3,2,1,0:T(2,128)(2,1)}), bf16[32,2,2,1024]{3,2,1,0:T(2,128)(2,1)S(1)}, u32[]{:S(2)}, u32[]{:S(2)}) async-start(bf16[32,2,2,1024]{3,2,1,0:T(2,128)(2,1)} %copy.35), calls=%async_computation.3 | async-start | bytes 524288 | tf_op jit(solution)/shard_map/all_to_all | solution.py:56
  146.5 263.8 %all-reduce.2.cloned.1.call-start = ((), (), s32[]{:S(2)}) async-start(), calls=%async_computation.6 | async-start | bytes 524288 | tf_op jit(solution)/shard_map/psum | solution.py:119
  146.5 3.6 copy-start.4
  152.2 9.4 %copy-start.2 = (bf16[1,256,1024]{2,1,0:T(8,128)(2,1)S(1)}, bf16[1,256,1024]{2,1,0:T(8,128)(2,1)}, u32[]{:S(2)}) copy-start(bf16[1,256,1024]{2,1,0:T(8,128)(2,1)} %param.5) | copy-start | bytes 1572868
  158.8 4.2 copy-start.6
Sparse Core Ops, SparseCore 0:
  38.8 36.3 all-gather.2
  83.3 14.5 reduce-scatter.2
  100.6 33.7 reduce-scatter.4
  163.1 247.1 all-reduce.1
where the time goes:
time: 419 us
  waiting for transfers between devices  339 us (81%)
  blocking collectives  25.9 us (6%)
  matrix products  21.6 us (5%)
  between operations  13.9 us (3%)
  starting transfers between devices  10.3 us (2%)
  local copies, waits for them, and re-layouts  7.79 us (2%)
    psum x1, waiting for transfers between devices, per_device(): grad_param = lax.psum(local_param, EX_EY)  245 us
    reduce_scatter x2, waiting for transfers between devices, sum_in_order(): tiles = lax.psum_scatter(tiles, axes[k], scatter_dimension=0, tiled=True)  51.1 us
    all_gather x1, waiting for transfers between devices, route_in(): return lax.all_gather(moved, EX, axis=0, tiled=True)  36.5 us
    all_to_all x1, blocking collectives, route_in(): lax.all_to_all(stacked, 'ey', split_axis=2, concat_axis=0, tiled=True)  25.9 us
    all_to_all x1, starting transfers between devices, route_out(): lax.all_to_all(summed.astype(jnp.bfloat16), 'ey', split_axis=0, concat_ax...  10.2 us
  transfers between devices with their start and end apart: 5, of which 5 were waited for; matrix products, arithmetic and copies ran while one was open for 2% of the time, Pallas kernels for 0%

commit v1 on v0

--- a/solution.py
+++ b/solution.py
@@ -6,6 +6,13 @@
 
 EX = ("ex_0", "ex_1")
 EX_EY = ("ex_0", "ex_1", "ey")
+
+
+def all_by_exchange(array, mesh_axis, dim):
+    peers = lax.axis_size(mesh_axis)
+    tiles = jnp.stack([array for _ in range(peers)])
+    tiles = lax.all_to_all(tiles, mesh_axis, split_axis=0, concat_axis=0)
+    return jnp.concatenate(tiles, axis=dim)
 
 
 def sum_in_order(tiles, axes, sequence):
@@ -41,7 +48,7 @@
 
 def route_in(stacked):
     moved = lax.all_to_all(stacked, "ey", split_axis=2, concat_axis=0, tiled=True)
-    return lax.all_gather(moved, EX, axis=0, tiled=True)
+    return all_by_exchange(moved, EX, 0)
 
 
 def route_out(term_fn, total_rows):

time: 419 us -> 430 us (1.026)
  blocking collectives: 25.9 us -> 80.2 us
  waiting for transfers between devices: 339 us -> 297 us
    all_to_all x0 -> x1, blocking collectives: none -> 54.3 us  [all_by_exchange(): tiles = lax.all_to_all(tiles, mesh_axis, split_axis=0, concat_axis=0)]
    all_gather x1 -> x0, waiting for transfers between devices: 36.5 us -> none  [route_in(): return lax.all_gather(moved, EX, axis=0, tiled=True)]
    reduce_scatter x2, waiting for transfers between devices: 51.1 us -> 46 us  [sum_in_order(): tiles = lax.psum_scatter(tiles, axes[k], scatter_dimension=0, tiled=True)]
  transfers between devices with their start and end apart: 5 -> 4, of which waited for: 5 -> 4; matrix products, arithmetic and copies ran while one was open for 2% -> 2% of each run, Pallas kernels for 0% -> 0%
where the time goes in v1:
time: 430 us
  waiting for transfers between devices  297 us (69%)
  blocking collectives  80.2 us (19%)
  matrix products  19.5 us (5%)
  between operations  13.9 us (3%)
  starting transfers between devices  10.3 us (2%)
  local copies, waits for them, and re-layouts  8.67 us (2%)
    psum x1, waiting for transfers between devices, per_device(): grad_param = lax.psum(local_param, EX_EY)  245 us
    all_to_all x1, blocking collectives, all_by_exchange(): tiles = lax.all_to_all(tiles, mesh_axis, split_axis=0, concat_axis=0)  54.3 us
    reduce_scatter x2, waiting for transfers between devices, sum_in_order(): tiles = lax.psum_scatter(tiles, axes[k], scatter_dimension=0, tiled=True)  46 us
    all_to_all x1, blocking collectives, route_in(): lax.all_to_all(stacked, 'ey', split_axis=2, concat_axis=0, tiled=True)  25.9 us
    all_to_all x1, starting transfers between devices, route_out(): lax.all_to_all(summed.astype(jnp.bfloat16), 'ey', split_axis=0, concat_ax...  10.2 us
  transfers between devices with their start and end apart: 4, of which 4 were waited for; matrix products, arithmetic and copies ran while one was open for 2% of the time, Pallas kernels for 0%

profile of v1, /device:TPU:2, one launch (start us, length us, event | category | flops | bytes accessed | tf_op | source)
XLA Modules:
  0.0 430.0 jit_solution(2312786111298335808)
XLA Ops:
  7.2 1.6 fusion.34
  8.8 0.2 fusion.23
  9.0 1.3 fusion.4
  10.3 1.2 fusion.5
  11.6 0.3 copy.24
  11.9 25.9 %all_to_all.38 = bf16[1,2,64,1024]{3,1,0,2:T(2,128)(2,1)S(1)} all-to-all(bf16[1,2,64,1024]{3,1,0,2:T(2,128)(2,1)S(1)} %copy.24), channel_id=1, replica_groups=mesh['ex_0'=4,'ex_1'=2,'ey'=32] {'ey'}, dimensions={2} | all-to-all | bytes 524288 | tf_op jit(solution)/shard_map/all_to_all | solution.py:50
  37.9 0.3 stack.26
  38.2 54.3 %all_to_all.39 = bf16[8,32,2,2,1024]{4,1,3,2,0:T(8,128)(2,1)S(1)} all-to-all(bf16[8,32,2,2,1024]{4,1,3,2,0:T(8,128)(2,1)S(1)} %stack.26), channel_id=1, replica_groups=mesh['ex_0'=4,'ex_1'=2,'ey'=32] {'ex_0','ex_1'}, dimensions={0} | all-to-all | bytes 4194304 | tf_op jit(solution)/shard_map/all_to_all | solution.py:14
  92.5 0.3 copy.26
  92.8 2.1 copy-done.3
  94.8 0.7 convolution_bitcast_fusion.1
  95.5 1.0 fusion.2
  96.5 0.7 convolution_convert_fusion.3
  97.3 0.7 convolution_convert_fusion.2
  98.1 0.2 pad_maximum_fusion
  98.3 1.5 copy.35
  99.8 9.5 %reduce-scatter.3.cloned.1.call-done = bf16[4,32,2,2,1024]{4,1,3,2,0:T(8,128)(2,1)} async-done(((bf16[8,32,2,2,1024]{4,1,3,2,0:T(8,128)(2,1)}), bf16[4,32,2,2,1024]{4,1,3,2,0:T(8,128)(2,1)}) %reduce-scatter.3.cloned.1.call-update) | async-done | bytes 1048592 | tf_op jit(solution)/shard_map/reduce_scatter | solution.py:23
  109.4 36.4 %reduce-scatter.5.cloned.1.call-done = bf16[1,32,2,2,1024]{4,1,3,2,0:T(8,128)(2,1)} async-done(((bf16[4,32,2,2,1024]{4,1,3,2,0:T(8,128)(2,1)}), bf16[1,32,2,2,1024]{4,1,3,2,0:T(8,128)(2,1)}) %reduce-scatter.5.cloned.1.call-update) | async-done | bytes 262160 | tf_op jit(solution)/shard_map/reduce_scatter | solution.py:23
  145.8 1.9 copy.29
  147.8 10.2 %all-to-all-start.2 = ((bf16[32,2,2,1024]{3,2,1,0:T(2,128)(2,1)}), bf16[32,2,2,1024]{3,2,1,0:T(2,128)(2,1)S(1)}, u32[]{:S(2)}, u32[]{:S(2)}) async-start(bf16[32,2,2,1024]{3,2,1,0:T(2,128)(2,1)} %copy.29), calls=%async_computation.4 | async-start | bytes 524288 | tf_op jit(solution)/shard_map/all_to_all | solution.py:63
  158.0 3.6 convolution_convert_fusion.1
  161.6 2.1 convolution_convert_fusion
  163.7 6.0 %all-to-all-done.2 = bf16[32,2,2,1024]{3,2,1,0:T(2,128)(2,1)S(1)} async-done(((bf16[32,2,2,1024]{3,2,1,0:T(2,128)(2,1)}), bf16[32,2,2,1024]{3,2,1,0:T(2,128)(2,1)S(1)}, u32[]{:S(2)}, u32[]{:S(2)}) %all-to-all-start.2) | async-done | bytes 262176 | tf_op jit(solution)/shard_map/all_to_all | solution.py:63
  169.7 0.2 copy.30
  169.9 0.4 fusion.35
  170.3 1.4 convolution_bitcast_fusion.3
  171.7 1.4 fusion.20
  173.1 0.4 multiply_reduce_fusion.1
  173.5 1.0 convolution_bitcast_fusion.2
  174.5 2.4 fusion.3
  176.9 244.8 %all-reduce.2.cloned.1.call-done = f32[1024,64]{0,1:T(8,128)} async-done(((f32[1024,64]{0,1:T(8,128)}), f32[1024,64]{0,1:T(8,128)}) %all-reduce.2.cloned.1.call-update) | async-done | bytes 262160 | tf_op jit(solution)/shard_map/psum | solution.py:126
  421.8 1.7 copy.53
  (21 shorter events, 0.4 us)
Async XLA Ops:
  7.2 88.4 %copy-start = (bf16[2,512,1024]{2,1,0:T(8,128)(2,1)S(1)}, bf16[2,512,1024]{2,1,0:T(8,128)(2,1)}, u32[]{:S(2)}) copy-start(bf16[2,512,1024]{2,1,0:T(8,128)(2,1)} %param.8) | copy-start | bytes 6291460
  7.2 102.2 %reduce-scatter.3.cloned.1.call-start = ((), (), s32[]{:S(2)}) async-start(), calls=%async_computation.5 | async-start | bytes 3145728 | tf_op jit(solution)/shard_map/reduce_scatter | solution.py:23
  92.5 2.3 copy-start.3
  92.7 2.8 copy-start.1
  96.5 0.8 copy-start.5
  99.8 46.0 %reduce-scatter.5.cloned.1.call-start = ((), (), s32[]{:S(2)}) async-start(), calls=%async_computation.6 | async-start | bytes 1310720 | tf_op jit(solution)/shard_map/reduce_scatter | solution.py:23
  147.8 22.0 %all-to-all-start.2 = ((bf16[32,2,2,1024]{3,2,1,0:T(2,128)(2,1)}), bf16[32,2,2,1024]{3,2,1,0:T(2,128)(2,1)S(1)}, u32[]{:S(2)}, u32[]{:S(2)}) async-start(bf16[32,2,2,1024]{3,2,1,0:T(2,128)(2,1)} %copy.29), calls=%async_computation.4 | async-start | bytes 524288 | tf_op jit(solution)/shard_map/all_to_all | solution.py:63
  157.9 263.8 %all-reduce.2.cloned.1.call-start = ((), (), s32[]{:S(2)}) async-start(), calls=%async_computation.7 | async-start | bytes 524288 | tf_op jit(solution)/shard_map/psum | solution.py:126
  158.0 3.6 copy-start.2
  163.7 9.4 %copy-start.4 = (bf16[1,256,1024]{2,1,0:T(8,128)(2,1)S(1)}, bf16[1,256,1024]{2,1,0:T(8,128)(2,1)}, u32[]{:S(2)}) copy-start(bf16[1,256,1024]{2,1,0:T(8,128)(2,1)} %param.5) | copy-start | bytes 1572868
  170.3 4.2 copy-start.6
Sparse Core Ops, SparseCore 0:
  99.9 9.4 reduce-scatter.2
  112.1 33.7 reduce-scatter.4
  174.6 247.1 all-reduce.1
